TPU v7x, 32 devices: a whole 2x2x4 slice. The times are simulated.
32 devices in a mesh: tile: 8 (over z, core), dp: 4 (over y, x).
Axes of the slice: x: 2, y: 2, z: 4, core: 2. Of those that a mesh axis runs over, the one named last changes fastest.
Arguments:
- clip_frames: bfloat16 [4, 8, 32, 8, 128], P('dp', None, 'tile'), may hold values from -6 to 6
- segments: int32 [4, 8], P('dp'), may hold values from 0 to 2, never falling along the last dimension, each value on 1 to 4 neighbouring positions
- weight_first: bfloat16 [3456, 128], replicated, may hold values from -0.109375 to 0.109375
- weight_second: bfloat16 [3456, 128], replicated, may hold values from -0.109375 to 0.109375
- cotangent: bfloat16 [4, 8, 16, 4, 128], P('dp', None, 'tile'), may hold values from -6 to 6
Outputs:
- pooled: float32 [4, 8, 16, 4, 128], P('dp', None, 'tile')
- input_grad: float32 [4, 8, 32, 8, 128], P('dp', None, 'tile')
- grad_first: float32 [3456, 128], P('tile')
- grad_second: float32 [3456, 128], P('tile')
Inputs may be any that keep to these rules, and one draw needn't show every extreme that they name: `segments`: clip numbers never fall along the frames of a sequence; each clip is one to 4 frames long and one clip has exactly 4.
All inputs are finite; a program needn't handle non-finite values.
Results may differ from a plain program's by a relative error of at most 0.0029.
Values may be sent and summed in bfloat16 or wider, within the bound.
A program may use at most 64 MiB of HBM per device.

v0:
```python
import math

import jax
import jax.numpy as jnp
from jax import lax
from jax.sharding import PartitionSpec as P


def padded_2(cells, sides, width):
    for axis, dim in sides:
        count = lax.axis_size(axis)
        ends = count - 1
        head = lax.slice_in_dim(cells, 0, width, axis=dim)
        tail = lax.slice_in_dim(cells, cells.shape[dim] - width, cells.shape[dim], axis=dim)
        cells = jnp.concatenate(
            [
                lax.ppermute(tail, axis, [(i, (i + 1) % count) for i in range(ends)]),
                cells,
                lax.ppermute(head, axis, [((i + 1) % count, i) for i in range(ends)]),
            ],
            axis=dim,
        )
    return cells


def make_masks(clip_ids):
    frame_count = clip_ids.shape[0]
    result = []
    for delay_step in range(3):
        earlier = jnp.concatenate(
            [jnp.full((delay_step,), -1, jnp.int32), clip_ids[: frame_count - delay_step]]
        )
        result.append(earlier == clip_ids)
    return result


def move_frames(field, delay_step, reverse):
    if delay_step == 0:
        return field
    filler = jnp.zeros((delay_step,) + field.shape[1:], field.dtype)
    if reverse:
        return jnp.concatenate([field[delay_step:], filler], axis=0)
    return jnp.concatenate([filler, field[: field.shape[0] - delay_step]], axis=0)


def tap_columns(padded, frame_masks, reverse, row_count, col_count):
    channels = padded.shape[-1]
    pieces = []
    for delay_step in range(3):
        keep = frame_masks[delay_step]
        if reverse:
            keep = move_frames(keep, delay_step, True)
        moved = jnp.where(
            keep[:, None, None, None],
            move_frames(padded, delay_step, reverse),
            jnp.zeros((), padded.dtype),
        )
        for row_tap in range(3):
            for col_tap in range(3):
                row_at = 2 - row_tap if reverse else row_tap
                col_at = 2 - col_tap if reverse else col_tap
                pieces.append(moved[:, row_at : row_at + row_count, col_at : col_at + col_count, :])
    return jnp.concatenate(pieces, axis=-1).reshape(-1, 27 * channels)


def flip_kernel(kernel):
    channels = kernel.shape[1]
    return (
        kernel.reshape(27, channels, channels).transpose(0, 2, 1).reshape(27 * channels, channels)
    )


def pad_cols(field):
    return jnp.pad(field, ((0, 0), (0, 0), (1, 1), (0, 0)))


def row_margin(field):
    return pad_cols(padded_2(field, (("tile", 1),), 1))


def local(clip_frames, segments, weight_first, weight_second, cotangent):
    frames_one = clip_frames[0]
    clip_ids = segments[0]
    cot_one = cotangent[0]
    frame_count, row_count, col_count, channels = frames_one.shape
    shape_four = (frame_count, row_count, col_count, channels)
    frame_masks = make_masks(clip_ids)
    columns_in = tap_columns(row_margin(frames_one), frame_masks, False, row_count, col_count)
    first_out = jnp.dot(columns_in, weight_first, preferred_element_type=jnp.float32)
    hidden = jax.nn.silu(first_out).astype(jnp.bfloat16).reshape(shape_four)
    columns_hidden = tap_columns(row_margin(hidden), frame_masks, False, row_count, col_count)
    second_out = jnp.dot(columns_hidden, weight_second, preferred_element_type=jnp.float32)
    summed = frames_one.astype(jnp.float32) + second_out.reshape(shape_four)
    pooled = summed.reshape(frame_count, row_count // 2, 2, col_count // 2, 2, channels).mean(
        axis=(2, 4)
    )
    cot_wide = padded_2(cot_one, (("tile", 1),), 1)
    grad_wide = jnp.repeat(jnp.repeat(cot_wide, 2, axis=1), 2, axis=2) * jnp.bfloat16(0.25)
    grad_padded = pad_cols(grad_wide[:, 1:-1])
    grad_out = grad_wide[:, 2:-2]
    columns_grad = tap_columns(grad_padded, frame_masks, True, row_count, col_count)
    grad_hidden = jnp.dot(
        columns_grad, flip_kernel(weight_second), preferred_element_type=jnp.float32
    )
    sigma = jax.nn.sigmoid(first_out)
    grad_act = (grad_hidden * sigma * (1.0 + first_out * (1.0 - sigma))).astype(jnp.bfloat16)
    act_padded = pad_cols(padded_2(grad_act.reshape(shape_four), (("tile", 1),), 1))
    columns_back = tap_columns(act_padded, frame_masks, True, row_count, col_count)
    back_term = jnp.dot(columns_back, flip_kernel(weight_first), preferred_element_type=jnp.float32)
    input_grad = grad_out.astype(jnp.float32) + back_term.reshape(shape_four)
    scale = 1.0 / math.sqrt(
        lax.axis_size("dp") * lax.axis_size("tile") * frame_count * row_count * col_count
    )
    local_second = (
        jnp.dot(
            columns_hidden.T, grad_out.reshape(-1, channels), preferred_element_type=jnp.float32
        )
        * scale
    )
    local_first = jnp.dot(columns_in.T, grad_act, preferred_element_type=jnp.float32) * scale
    share_first, share_second = (
        lax.psum_scatter(local_first, "tile", scatter_dimension=0, tiled=True),
        lax.psum_scatter(local_second, "tile", scatter_dimension=0, tiled=True),
    )
    grad_first, grad_second = lax.psum((share_first, share_second), "dp")
    return (pooled[None], input_grad[None], grad_first, grad_second)


def solution(mesh):
    return jax.shard_map(
        local,
        mesh=mesh,
        in_specs=(
            P("dp", None, "tile", None, None),
            P("dp", None),
            P(),
            P(),
            P("dp", None, "tile", None, None),
        ),
        out_specs=(
            P("dp", None, "tile", None, None),
            P("dp", None, "tile", None, None),
            P("tile", None),
            P("tile", None),
        ),
        check_vma=False,
    )
```

profile of v0, /device:TPU:0, one launch (start us, length us, event | category | flops | bytes accessed | tf_op | source)
XLA Modules:
  0.0 160.5 jit_solution(13072548899679170073)
XLA Ops:
  7.2 0.8 fusion.18
  8.0 2.3 %collective-permute-start.4 = (bf16[8,1,4,128]{3,2,1,0:T(4,128)(2,1)S(1)}, bf16[8,1,4,128]{3,2,1,0:T(4,128)(2,1)S(1)}, u32[]{:S(2)}, u32[]{:S(2)}) collective-permute-start(bf16[8,1,4,128]{3,2,1,0:T(4,128)(2,1)S(1)} %get-tuple-element.38), channel_id=1, source_target_pairs={{0,4},{4,8},{8,12},{12,16},{16,20},{20,24},{24,28},{1,5},{5,9},{9,... | collective-permute-start | bytes 24584 | tf_op jit(solution)/shard_map/ppermute | solution.py:17
  10.4 1.3 collective-permute-start.5
  11.7 0.7 fusion.17
  12.4 5.2 %collective-permute-start = (bf16[8,1,8,128]{3,2,1,0:T(8,128)(2,1)S(1)}, bf16[8,1,8,128]{3,2,1,0:T(8,128)(2,1)S(1)}, u32[]{:S(2)}, u32[]{:S(2)}) collective-permute-start(bf16[8,1,8,128]{3,2,1,0:T(8,128)(2,1)S(1)} %get-tuple-element.36), channel_id=1, source_target_pairs={{0,4},{4,8},{8,12},{12,16},{16,20},{20,24},{24,28},{1,5},{5,9},{9,... | collective-permute-start | bytes 49160 | tf_op jit(solution)/shard_map/ppermute | solution.py:17
  17.6 1.3 collective-permute-start.1
  18.9 0.7 slice_bitcast_fusion
  19.6 0.7 slice_bitcast_fusion.1
  20.2 0.7 bitcast_compare_fusion
  21.2 1.9 %copy.11 = bf16[27,128,128]{2,1,0:T(8,128)(2,1)S(1)} copy(bf16[27,128,128]{1,2,0:T(8,128)(2,1)} %bitcast.80) | data formatting | bytes 1769472 | tf_op jit(solution)/shard_map/transpose | solution.py:69
  23.1 1.3 copy.12
  28.5 1.9 %convolution_multiply_fusion = f32[3456,128]{1,0:T(8,128)} fusion(bf16[256,3456]{1,0:T(8,128)(2,1)S(1)} %constant_dynamic-update-slice_fusion, bf16[256,128]{1,0:T(8,128)(2,1)S(1)} %fusion.3), kind=kOutput, calls=%fused_computation | convolution fusion | flops 226934784 | bytes 3604480 | tf_op jit(solution)/shard_map/dot_general | solution.py:120
  30.5 4.3 %collective-permute-start.2 = (bf16[8,1,8,128]{3,2,1,0:T(8,128)(2,1)S(1)}, bf16[8,1,8,128]{3,2,1,0:T(8,128)(2,1)S(1)}, u32[]{:S(2)}, u32[]{:S(2)}) collective-permute-start(bf16[8,1,8,128]{3,2,1,0:T(8,128)(2,1)S(1)} %get-tuple-element.32), channel_id=1, source_target_pairs={{0,4},{4,8},{8,12},{12,16},{16,20},{20,24},{24,28},{1,5},{5,9},{9,... | collective-permute-start | bytes 49160 | tf_op jit(solution)/shard_map/ppermute | solution.py:17
  34.8 1.3 collective-permute-start.3
  36.1 4.3 %collective-permute-start.6 = (bf16[8,1,8,128]{3,2,1,0:T(8,128)(2,1)S(1)}, bf16[8,1,8,128]{3,2,1,0:T(8,128)(2,1)S(1)}, u32[]{:S(2)}, u32[]{:S(2)}) collective-permute-start(bf16[8,1,8,128]{3,2,1,0:T(8,128)(2,1)S(1)} %get-tuple-element.30), channel_id=1, source_target_pairs={{0,4},{4,8},{8,12},{12,16},{16,20},{20,24},{24,28},{1,5},{5,9},{9,... | collective-permute-start | bytes 49160 | tf_op jit(solution)/shard_map/ppermute | solution.py:17
  40.4 1.3 collective-permute-start.7
  42.8 2.0 %collective-permute-done.7 = bf16[8,1,8,128]{3,2,1,0:T(8,128)(2,1)S(1)} collective-permute-done((bf16[8,1,8,128]{3,2,1,0:T(8,128)(2,1)S(1)}, bf16[8,1,8,128]{3,2,1,0:T(8,128)(2,1)S(1)}, u32[]{:S(2)}, u32[]{:S(2)}) %collective-permute-start.7) | collective-permute-done | bytes 16416 | tf_op jit(solution)/shard_map/ppermute | solution.py:19
  46.2 2.0 %fusion = f32[3456,128]{1,0:T(8,128)} fusion(bf16[8,4,8,3456]{3,2,1,0:T(8,128)(2,1)S(1)} %constant_dynamic-update-slice_fusion.27, bf16[8,8,8,128]{3,2,1,0:T(8,128)(2,1)S(1)} %bitcast.91), kind=kOutput, calls=%fused_computation.2 | convolution fusion | flops 226934784 | bytes 3604480 | tf_op jit(solution)/shard_map/dot_general | solution.py:115
  49.6 19.7 %reduce-scatter.3.cloned.1.call-done = f32[432,128]{1,0:T(8,128)} async-done(((f32[3456,128]{1,0:T(8,128)}), f32[432,128]{1,0:T(8,128)}) %reduce-scatter.3.cloned.1.call-update) | async-done | bytes 221200 | tf_op jit(solution)/shard_map/reduce_scatter | solution.py:122
  69.3 35.5 %reduce-scatter.5.cloned.1.call-done = f32[432,128]{1,0:T(8,128)} async-done(((f32[3456,128]{1,0:T(8,128)}), f32[432,128]{1,0:T(8,128)}) %reduce-scatter.5.cloned.1.call-update) | async-done | bytes 221200 | tf_op jit(solution)/shard_map/reduce_scatter | solution.py:123
  105.4 1.3 fusion.1
  106.7 44.0 %all-reduce.17.cloned.1.call-done = (f32[432,128]{1,0:T(8,128)}, f32[432,128]{1,0:T(8,128)}) async-done(((f32[432,128]{1,0:T(8,128)}, f32[432,128]{1,0:T(8,128)}), (f32[432,128]{1,0:T(8,128)}, f32[432,128]{1,0:T(8,128)})) %all-reduce.17.cloned.1.call-update) | async-done | bytes 442384 | tf_op jit(solution)/shard_map/psum | solution.py:125
  150.7 1.6 %copy.122 = f32[432,128]{1,0:T(8,128)} copy(f32[432,128]{1,0:T(8,128)} %get-tuple-element.48) | data formatting | bytes 442368
  152.3 1.6 %copy.123 = f32[432,128]{1,0:T(8,128)} copy(f32[432,128]{1,0:T(8,128)} %get-tuple-element.49) | data formatting | bytes 442368
  (169 shorter events, 8.1 us)
Async XLA Ops:
  7.2 16.0 %copy-start.3 = (bf16[3456,128]{1,0:T(8,128)(2,1)S(1)}, bf16[3456,128]{1,0:T(8,128)(2,1)}, u32[]{:S(2)}) copy-start(bf16[3456,128]{1,0:T(8,128)(2,1)} %param.7) | copy-start | bytes 2654212
  7.2 62.1 %reduce-scatter.3.cloned.1.call-start = ((), (), s32[]{:S(2)}) async-start(), calls=%async_computation.2 | async-start | bytes 1990656 | tf_op jit(solution)/shard_map/reduce_scatter | solution.py:122
  8.0 16.5 %collective-permute-start.4 = (bf16[8,1,4,128]{3,2,1,0:T(4,128)(2,1)S(1)}, bf16[8,1,4,128]{3,2,1,0:T(4,128)(2,1)S(1)}, u32[]{:S(2)}, u32[]{:S(2)}) collective-permute-start(bf16[8,1,4,128]{3,2,1,0:T(4,128)(2,1)S(1)} %get-tuple-element.38), channel_id=1, source_target_pairs={{0,4},{4,8},{8,12},{12,16},{16,20},{20,24},{24,28},{1,5},{5,9},{9,... | collective-permute-start | bytes 24584 | tf_op jit(solution)/shard_map/ppermute | solution.py:17
  10.4 14.1 %collective-permute-start.5 = (bf16[8,1,4,128]{3,2,1,0:T(4,128)(2,1)S(1)}, bf16[8,1,4,128]{3,2,1,0:T(4,128)(2,1)S(1)}, u32[]{:S(2)}, u32[]{:S(2)}) collective-permute-start(bf16[8,1,4,128]{3,2,1,0:T(4,128)(2,1)S(1)} %get-tuple-element.39), channel_id=1, source_target_pairs={{4,0},{8,4},{12,8},{16,12},{20,16},{24,20},{28,24},{5,1},{9,5},{13... | collective-permute-start | bytes 24584 | tf_op jit(solution)/shard_map/ppermute | solution.py:19
  12.4 13.5 %collective-permute-start = (bf16[8,1,8,128]{3,2,1,0:T(8,128)(2,1)S(1)}, bf16[8,1,8,128]{3,2,1,0:T(8,128)(2,1)S(1)}, u32[]{:S(2)}, u32[]{:S(2)}) collective-permute-start(bf16[8,1,8,128]{3,2,1,0:T(8,128)(2,1)S(1)} %get-tuple-element.36), channel_id=1, source_target_pairs={{0,4},{4,8},{8,12},{12,16},{16,20},{20,24},{24,28},{1,5},{5,9},{9,... | collective-permute-start | bytes 49160 | tf_op jit(solution)/shard_map/ppermute | solution.py:17
  17.6 8.3 %collective-permute-start.1 = (bf16[8,1,8,128]{3,2,1,0:T(8,128)(2,1)S(1)}, bf16[8,1,8,128]{3,2,1,0:T(8,128)(2,1)S(1)}, u32[]{:S(2)}, u32[]{:S(2)}) collective-permute-start(bf16[8,1,8,128]{3,2,1,0:T(8,128)(2,1)S(1)} %get-tuple-element.37), channel_id=1, source_target_pairs={{4,0},{8,4},{12,8},{16,12},{20,16},{24,20},{28,24},{5,1},{9,5},{13... | collective-permute-start | bytes 49160 | tf_op jit(solution)/shard_map/ppermute | solution.py:19
  21.2 3.3 %copy-start.4 = (bf16[1,8,2,4,128]{4,3,2,1,0:T(4,128)(2,1)S(1)}, bf16[1,8,2,4,128]{4,3,2,1,0:T(4,128)(2,1)}, u32[]{:S(2)}) copy-start(bf16[1,8,2,4,128]{4,3,2,1,0:T(4,128)(2,1)} %param.9) | copy-start | bytes 49156
  25.0 1.0 copy-start.2
  30.5 74.3 %reduce-scatter.5.cloned.1.call-start = ((), (), s32[]{:S(2)}) async-start(), calls=%async_computation.3 | async-start | bytes 1990656 | tf_op jit(solution)/shard_map/reduce_scatter | solution.py:123
  30.5 11.2 %collective-permute-start.2 = (bf16[8,1,8,128]{3,2,1,0:T(8,128)(2,1)S(1)}, bf16[8,1,8,128]{3,2,1,0:T(8,128)(2,1)S(1)}, u32[]{:S(2)}, u32[]{:S(2)}) collective-permute-start(bf16[8,1,8,128]{3,2,1,0:T(8,128)(2,1)S(1)} %get-tuple-element.32), channel_id=1, source_target_pairs={{0,4},{4,8},{8,12},{12,16},{16,20},{20,24},{24,28},{1,5},{5,9},{9,... | collective-permute-start | bytes 49160 | tf_op jit(solution)/shard_map/ppermute | solution.py:17
  34.8 6.9 %collective-permute-start.3 = (bf16[8,1,8,128]{3,2,1,0:T(8,128)(2,1)S(1)}, bf16[8,1,8,128]{3,2,1,0:T(8,128)(2,1)S(1)}, u32[]{:S(2)}, u32[]{:S(2)}) collective-permute-start(bf16[8,1,8,128]{3,2,1,0:T(8,128)(2,1)S(1)} %get-tuple-element.33), channel_id=1, source_target_pairs={{4,0},{8,4},{12,8},{16,12},{20,16},{24,20},{28,24},{5,1},{9,5},{13... | collective-permute-start | bytes 49160 | tf_op jit(solution)/shard_map/ppermute | solution.py:19
  36.1 6.6 %collective-permute-start.6 = (bf16[8,1,8,128]{3,2,1,0:T(8,128)(2,1)S(1)}, bf16[8,1,8,128]{3,2,1,0:T(8,128)(2,1)S(1)}, u32[]{:S(2)}, u32[]{:S(2)}) collective-permute-start(bf16[8,1,8,128]{3,2,1,0:T(8,128)(2,1)S(1)} %get-tuple-element.30), channel_id=1, source_target_pairs={{0,4},{4,8},{8,12},{12,16},{16,20},{20,24},{24,28},{1,5},{5,9},{9,... | collective-permute-start | bytes 49160 | tf_op jit(solution)/shard_map/ppermute | solution.py:17
  40.4 4.3 %collective-permute-start.7 = (bf16[8,1,8,128]{3,2,1,0:T(8,128)(2,1)S(1)}, bf16[8,1,8,128]{3,2,1,0:T(8,128)(2,1)S(1)}, u32[]{:S(2)}, u32[]{:S(2)}) collective-permute-start(bf16[8,1,8,128]{3,2,1,0:T(8,128)(2,1)S(1)} %get-tuple-element.31), channel_id=1, source_target_pairs={{4,0},{8,4},{12,8},{16,12},{20,16},{24,20},{28,24},{5,1},{9,5},{13... | collective-permute-start | bytes 49160 | tf_op jit(solution)/shard_map/ppermute | solution.py:19
  42.7 2.8 %copy-start.1 = (bf16[3456,128]{1,0:T(8,128)(2,1)S(1)}, bf16[3456,128]{1,0:T(8,128)(2,1)}, u32[]{:S(2)}) copy-start(bf16[3456,128]{1,0:T(8,128)(2,1)} %param.8) | copy-start | bytes 2654212
  44.8 1.4 copy-start
  48.2 0.9 slice-start
  48.3 102.4 %all-reduce.17.cloned.1.call-start = ((), (), s32[]{:S(2)}) async-start(), calls=%async_computation.4 | async-start | bytes 884736 | tf_op jit(solution)/shard_map/psum | solution.py:125
Sparse Core Ops, SparseCore 0:
  30.6 38.6 reduce-scatter.2
  71.6 33.1 reduce-scatter.4
  107.9 42.7 all-reduce.16
where the time goes:
time: 161 us; the launch traced here: 160 us
  waiting for transfers between devices  101 us (63%)
  starting transfers between devices  21.4 us (13%)
  between operations  14.6 us (9%)
  local copies, waits for them, and re-layouts  13.6 us (8%)
  matrix products  7.13 us (4%)
  other arithmetic  2.55 us (2%)
    psum x1, waiting for transfers between devices, local(): grad_first, grad_second = lax.psum((share_first, share_second), 'dp')  44 us
    reduce_scatter x1, waiting for transfers between devices, local(): lax.psum_scatter(local_second, 'tile', scatter_dimension=0, tiled=True)  35.5 us
    reduce_scatter x1, waiting for transfers between devices, local(): lax.psum_scatter(local_first, 'tile', scatter_dimension=0, tiled=True)  19.7 us
    ppermute x4, starting transfers between devices, padded_2(): lax.ppermute(tail, axis, [(i, (i + 1) % count) for i in range(ends)])  16.1 us
    unnamed x112, local copies, waits for them, and re-layouts  6.21 us
    ppermute x4, starting transfers between devices, padded_2(): lax.ppermute(head, axis, [((i + 1) % count, i) for i in range(ends)])  5.17 us
  transfers between devices with their start and end apart: 11, of which 4 were waited for; matrix products, arithmetic and copies ran while one was open for 9% of the time, Pallas kernels for 0%

commit v1 on v0

v1 whole, which is shorter than its diff:
```python
import functools
import math

import jax
import jax.numpy as jnp
from jax import lax
from jax.experimental import pallas as pl
from jax.experimental.pallas import tpu as pltpu
from jax.sharding import PartitionSpec as P

MESH = pl.DeviceIdType.MESH
F32 = jnp.float32
BF16 = jnp.bfloat16


def up16(n):
    return -(-n // 16) * 16


def shifted_cols(cells, step):
    if step == 0:
        return cells
    cols = cells.shape[2]
    col = lax.broadcasted_iota(jnp.int32, cells.shape, 2)
    moved = pltpu.roll(cells, (-step) % cols, 2)
    keep = (col < cols - 1) if step == 1 else (col > 0)
    return jnp.where(keep, moved, 0.0)


def fill_columns(dst, cells, same, reverse):
    rows, frames, cols, ch = cells.shape
    for ci in range(3):
        moved = shifted_cols(cells, (1 - ci) if reverse else (ci - 1))
        for t in range(3):
            zero = jnp.zeros((rows, cols, ch), F32)
            parts = []
            for f in range(frames):
                src = f + t if reverse else f - t
                if src < 0 or src >= frames:
                    parts.append(zero)
                elif t == 0:
                    parts.append(moved[:, src])
                else:
                    parts.append(moved[:, src] * same[t][max(f, src)])
            block = jnp.stack(parts, axis=1).reshape(rows * frames * cols, ch)
            at = (t * 3 + ci) * ch
            dst[:, at : at + ch] = block.astype(BF16)


def conv_dots(cols_ref, w_ref, start, rows, slab, reverse):
    acc = None
    span = w_ref.shape[1] * 3
    for t in range(3):
        for a in range(3):
            at = (start + (2 - a if reverse else a)) * slab
            term = jnp.dot(
                cols_ref[at : at + rows * slab, t * span : (t + 1) * span],
                w_ref[(t * 3 + a) * span : (t * 3 + a + 1) * span, :],
                preferred_element_type=F32,
            )
            acc = term if acc is None else acc + term
    return acc


def kernel(
    cfg,
    seg, x_in, w1, w2, g_in,
    pooled, in_grad, out1, out2,
    x_halo, g_halo, cols_x, cols_h, cols_g, cols_a, w1t, w2t, pool_tmp,
    flat1, flat2, recv_a, sum_a, send_b, recv_b, sum_b, send_c, recv_c, fin,
    h_send, h_recv, a_send, a_recv, b_send, b_recv, c_send, c_recv, d_send, d_recv,
):
    n_tile, n_dp, share, chunk, scale = cfg
    n_z = n_tile // 2
    rows, slab, ch = x_in.shape
    frames = seg.shape[1]
    cols = slab // frames
    tile = lax.axis_index("tile")
    dp = lax.axis_index("dp")
    core = lax.rem(tile, 2)
    z = lax.div(tile, 2)
    flats = (flat1, flat2)
    outs = (out1, out2)

    barrier = pltpu.get_barrier_semaphore()

    def greet(peer):
        pl.semaphore_signal(barrier, inc=1, device_id=peer, device_id_type=MESH)

    @pl.when(tile > 0)
    def _():
        greet({"tile": tile - 1})

    @pl.when(tile < n_tile - 1)
    def _():
        greet({"tile": tile + 1})

    for i in range(1, n_dp):
        greet({"dp": lax.rem(dp + i, n_dp)})
    for j in range(1, n_z):
        greet({"tile": 2 * lax.rem(z + j, n_z) + core})

    span = 3 * ch

    def flip(src, dst):
        for tap in range(27):
            dst[tap * ch : (tap + 1) * ch, :] = src[tap * ch : (tap + 1) * ch, :].T

    flip(w2, w2t)
    for g in range(2):
        sum_a[g, :, share:, :] = jnp.zeros((n_z, sum_a.shape[2] - share, ch), F32)

    @pl.when(tile == 0)
    def _():
        x_halo[0] = jnp.zeros(x_halo.shape[1:], BF16)
        g_halo[0] = jnp.zeros(g_halo.shape[1:], BF16)

    @pl.when(tile == n_tile - 1)
    def _():
        x_halo[1] = jnp.zeros(x_halo.shape[1:], BF16)
        g_halo[1] = jnp.zeros(g_halo.shape[1:], BF16)

    beside = jnp.where(tile > 0, 1, 0) + jnp.where(tile < n_tile - 1, 1, 0)
    pl.semaphore_wait(barrier, n_dp - 1 + n_z - 1 + beside)

    g_rows = g_in.shape[0]

    def halo(side):
        peer = {"tile": tile - 1 if side == 0 else tile + 1}
        return (
            pltpu.make_async_remote_copy(
                src_ref=x_in.at[0:2] if side == 0 else x_in.at[rows - 2 : rows],
                dst_ref=x_halo.at[1 - side],
                send_sem=h_send.at[side], recv_sem=h_recv.at[1 - side],
                device_id=peer, device_id_type=MESH,
            ),
            pltpu.make_async_remote_copy(
                src_ref=g_in.at[0:1] if side == 0 else g_in.at[g_rows - 1 : g_rows],
                dst_ref=g_halo.at[1 - side],
                send_sem=h_send.at[2 + side], recv_sem=h_recv.at[2 + 1 - side],
                device_id=peer, device_id_type=MESH,
            ),
        )

    @pl.when(tile > 0)
    def _():
        for copy in halo(0):
            copy.start()

    @pl.when(tile < n_tile - 1)
    def _():
        for copy in halo(1):
            copy.start()

    flip(w1, w1t)
    same = [None]
    for t in range(1, 3):
        same.append(
            [None] * t
            + [jnp.where(seg[0, f] == seg[0, f - t], 1.0, 0.0).astype(F32) for f in range(t, frames)]
        )

    @pl.when(tile > 0)
    def _():
        for copy in halo(0):
            copy.wait_send()
        for copy in halo(1):
            copy.wait_recv()

    @pl.when(tile < n_tile - 1)
    def _():
        for copy in halo(1):
            copy.wait_send()
        for copy in halo(0):
            copy.wait_recv()

    def four(v):
        return v.reshape(v.shape[0], frames, cols, ch)

    mine = x_in[...].astype(F32)
    x_all = jnp.concatenate([x_halo[0].astype(F32), mine, x_halo[1].astype(F32)], axis=0)
    fill_columns(cols_x, four(x_all), same, False)
    g_all = jnp.concatenate([g_halo[0], g_in[...], g_halo[1]], axis=0).astype(F32)
    g_all = jnp.stack([g_all, g_all], axis=1).reshape(2 * g_all.shape[0], slab, ch)
    fill_columns(cols_g, four(g_all), same, True)

    wide = rows + 2
    first = conv_dots(cols_x, w1, 0, wide, slab, False)
    sigma = 1.0 / (1.0 + jnp.exp(-first))
    top = jnp.where(tile > 0, 1.0, 0.0).astype(F32)
    low = jnp.where(tile < n_tile - 1, 1.0, 0.0).astype(F32)

    def edges(v):
        v = v.reshape(wide, slab, ch)
        return jnp.concatenate([v[:1] * top, v[1:-1], v[-1:] * low], axis=0)

    hidden_grad = conv_dots(cols_g, w2t, 0, wide, slab, True)
    act = edges(hidden_grad * sigma * (1.0 + first * (1.0 - sigma)))
    act_own = act[1 : 1 + rows].reshape(rows * slab, ch).astype(BF16)

    def kernel_grad(flat, cols_ref, start, g):
        for t in range(3):
            for a in range(3):
                at = (start + a) * slab
                flat[(t * 3 + a) * span : (t * 3 + a + 1) * span, :] = lax.dot_general(
                    cols_ref[at : at + rows * slab, t * span : (t + 1) * span],
                    g,
                    (((0,), (0,)), ((), ())),
                    preferred_element_type=F32,
                )

    def copies_a(g):
        return [
            pltpu.make_async_remote_copy(
                src_ref=flats[g].at[pl.ds(pl.multiple_of((2 * k + 1 - core) * share, 8), share)],
                dst_ref=recv_a.at[g, k],
                send_sem=a_send.at[g, k], recv_sem=a_recv.at[g, k],
                device_id={"tile": tile + 1 - 2 * core}, device_id_type=MESH,
            )
            for k in range(n_z)
        ]

    def copies_b(g):
        return [
            pltpu.make_async_remote_copy(
                src_ref=send_b.at[g, i - 1], dst_ref=recv_b.at[g, i - 1],
                send_sem=b_send.at[g, i - 1], recv_sem=b_recv.at[g, i - 1],
                device_id={"dp": lax.rem(dp + i, n_dp)}, device_id_type=MESH,
            )
            for i in range(1, n_dp)
        ]

    def copies_c(g):
        return [
            pltpu.make_async_remote_copy(
                src_ref=send_c.at[g, j - 1], dst_ref=recv_c.at[g, j - 1],
                send_sem=c_send.at[g, j - 1], recv_sem=c_recv.at[g, j - 1],
                device_id={"tile": 2 * lax.rem(z + j, n_z) + core}, device_id_type=MESH,
            )
            for j in range(1, n_z)
        ]

    def part(q):
        return pl.ds(pl.multiple_of(q * chunk, 16), chunk)

    def copies_d(g):
        return [
            pltpu.make_async_remote_copy(
                src_ref=fin.at[g, part(dp)], dst_ref=fin.at[g, part(dp)],
                send_sem=d_send.at[g, i - 1], recv_sem=d_recv.at[g, i - 1],
                device_id={"dp": lax.rem(dp + i, n_dp)}, device_id_type=MESH,
            )
            for i in range(1, n_dp)
        ]

    def start(copies):
        for copy in copies:
            copy.start()

    def wait(copies):
        for copy in copies:
            copy.wait()

    def step_b(g):
        wait(copies_a(g))
        for k in range(n_z):
            own = flats[g][pl.ds(pl.multiple_of((2 * k + core) * share, 8), share), :]
            sum_a[g, k, 0:share, :] = own + recv_a[g, k]
        for i in range(1, n_dp):
            send_b[g, i - 1] = sum_a[g, :, part(lax.rem(dp + i, n_dp)), :].astype(BF16)
        start(copies_b(g))

    def step_c(g):
        wait(copies_b(g))
        total = sum_a[g, :, part(dp), :]
        for i in range(1, n_dp):
            total = total + recv_b[g, i - 1].astype(F32)
        sum_b[g] = total
        for j in range(1, n_z):
            send_c[g, j - 1] = sum_b[g, lax.rem(z + j, n_z)].astype(BF16)
        start(copies_c(g))

    def step_d(g):
        wait(copies_c(g))
        total = sum_b[g, z]
        for j in range(1, n_z):
            total = total + recv_c[g, j - 1].astype(F32)
        fin[g, part(dp), :] = total * scale
        start(copies_d(g))

    kernel_grad(flat1, cols_x, 1, act_own)
    start(copies_a(0))
    hidden = edges(first * sigma)
    fill_columns(cols_h, four(hidden), same, False)
    g_own = g_all[2 : 2 + rows].reshape(rows * slab, ch)
    kernel_grad(flat2, cols_h, 0, g_own.astype(BF16))
    start(copies_a(1))
    step_b(0)
    step_b(1)
    second = conv_dots(cols_h, w2, 0, rows, slab, False)
    summed = mine + second.reshape(rows, slab, ch)
    pairs = rows // 2
    for i in range(pairs):
        pool_tmp[i * slab : (i + 1) * slab, :] = summed[2 * i] + summed[2 * i + 1]
    half = pairs * slab // 2
    pooled[...] = 0.25 * (
        pool_tmp[pl.ds(0, half, stride=2), :] + pool_tmp[pl.ds(1, half, stride=2), :]
    )
    fill_columns(cols_a, four(act), same, True)
    step_c(0)
    back = conv_dots(cols_a, w1t, 0, rows, slab, True)
    in_grad[...] = g_own + back
    step_c(1)
    step_d(0)
    step_d(1)
    for g in range(2):
        wait(copies_d(g))
        outs[g][...] = fin[g, 0:share, :]


def local(n_tile, n_dp, clip_frames, segments, weight_first, weight_second, cotangent):
    _, frames, rows, cols, ch = clip_frames.shape
    slab = frames * cols
    taps = weight_first.shape[0]
    share = taps // n_tile
    chunk = up16(-(-share // n_dp))
    n_z = n_tile // 2
    x = clip_frames[0].transpose(1, 0, 2, 3).reshape(rows, slab, ch)
    g = jnp.repeat(cotangent[0].transpose(1, 0, 2, 3), 2, axis=2) * jnp.bfloat16(0.25)
    g = g.reshape(rows // 2, slab, ch)
    scale = 1.0 / math.sqrt(n_dp * n_tile * rows * slab)
    vmem = pl.BlockSpec(memory_space=pltpu.VMEM)
    cells = rows * slab
    sem = pltpu.SemaphoreType.DMA
    pooled, in_grad, first, second = pl.pallas_call(
        functools.partial(kernel, (n_tile, n_dp, share, chunk, scale)),
        out_shape=(
            jax.ShapeDtypeStruct((cells // 4, ch), F32),
            jax.ShapeDtypeStruct((cells, ch), F32),
            jax.ShapeDtypeStruct((share, ch), F32),
            jax.ShapeDtypeStruct((share, ch), F32),
        ),
        in_specs=[pl.BlockSpec(memory_space=pltpu.SMEM)] + [vmem] * 4,
        out_specs=(vmem,) * 4,
        scratch_shapes=[
            pltpu.VMEM((2, 2, slab, ch), BF16),
            pltpu.VMEM((2, 1, slab, ch), BF16),
            pltpu.VMEM(((rows + 4) * slab, 9 * ch), BF16),
            pltpu.VMEM(((rows + 2) * slab, 9 * ch), BF16),
            pltpu.VMEM(((rows + 4) * slab, 9 * ch), BF16),
            pltpu.VMEM(((rows + 2) * slab, 9 * ch), BF16),
            pltpu.VMEM((taps, ch), BF16),
            pltpu.VMEM((taps, ch), BF16),
            pltpu.VMEM((cells // 2, ch), F32),
            pltpu.VMEM((taps, ch), F32),
            pltpu.VMEM((taps, ch), F32),
            pltpu.VMEM((2, n_z, share, ch), F32),
            pltpu.VMEM((2, n_z, n_dp * chunk, ch), F32),
            pltpu.VMEM((2, n_dp - 1, n_z, chunk, ch), BF16),
            pltpu.VMEM((2, n_dp - 1, n_z, chunk, ch), BF16),
            pltpu.VMEM((2, n_z, chunk, ch), F32),
            pltpu.VMEM((2, n_z - 1, chunk, ch), BF16),
            pltpu.VMEM((2, n_z - 1, chunk, ch), BF16),
            pltpu.VMEM((2, n_dp * chunk, ch), F32),
            sem((4,)), sem((4,)),
            sem((2, n_z)), sem((2, n_z)),
            sem((2, n_dp - 1)), sem((2, n_dp - 1)),
            sem((2, n_z - 1)), sem((2, n_z - 1)),
            sem((2, n_dp - 1)), sem((2, n_dp - 1)),
        ],
        compiler_params=pltpu.CompilerParams(
            collective_id=0, has_side_effects=True, vmem_limit_bytes=50 * 1024 * 1024
        ),
    )(segments, x, weight_first, weight_second, g)
    pooled = pooled.reshape(rows // 2, frames, cols // 2, ch).transpose(1, 0, 2, 3)
    in_grad = in_grad.reshape(rows, frames, cols, ch).transpose(1, 0, 2, 3)
    return (pooled[None], in_grad[None], first, second)


def solution(mesh):
    return jax.shard_map(
        functools.partial(local, mesh.shape["tile"], mesh.shape["dp"]),
        mesh=mesh,
        in_specs=(
            P("dp", None, "tile", None, None),
            P("dp", None),
            P(),
            P(),
            P("dp", None, "tile", None, None),
        ),
        out_specs=(
            P("dp", None, "tile", None, None),
            P("dp", None, "tile", None, None),
            P("tile", None),
            P("tile", None),
        ),
        check_vma=False,
    )
```

time: 161 us -> 41.4 us (0.26)
  waiting for transfers between devices: 101 us -> 0 us
  Pallas kernels: 0 us -> 34 us
  starting transfers between devices: 21.4 us -> 0 us
  between operations: 14.6 us -> 0.68 us
  local copies, waits for them, and re-layouts: 13.6 us -> 5.7 us
  matrix products: 7.13 us -> 0 us
  other arithmetic: 2.55 us -> 0.76 us
    reduce_scatter x2 -> x0, waiting for transfers between devices: 55.2 us -> none  [the longest x1 35.5 us: local(): lax.psum_scatter(local_second, 'tile', scatter_dimension=0, tiled=True)]
    psum x1 -> x0, waiting for transfers between devices: 44 us -> none  [local(): grad_first, grad_second = lax.psum((share_first, share_second), 'dp')]
    pallas_call x0 -> x1, Pallas kernels: none -> 34 us  [local(): pl.pallas_call(functools.partial(kernel, (n_tile, n_dp, share, chunk, sca...]
    ppermute x8 -> x0, starting transfers between devices: 21.3 us -> none  [the longest x4 16.1 us: padded_2(): lax.ppermute(tail, axis, [(i, (i + 1) % count) for i in range(ends)])]
    dot_general x6 -> x0, matrix products: 7.13 us -> none  [the longest x1 2.04 us: local(): jnp.dot(columns_hidden.T, grad_out.reshape(-1, channels), preferred_eleme...]
    slice x20 -> x0, local copies, waits for them, and re-layouts: 3.26 us -> none  [the longest x4 1.55 us: padded_2(): lax.slice_in_dim(cells, cells.shape[dim] - width, cells.shape[dim], axis=...]
    transpose x2 -> x0, local copies, waits for them, and re-layouts: 3.21 us -> none  [flip_kernel(): kernel.reshape(27, channels, channels).transpose(0, 2, 1)]
    ppermute x8 -> x0, waiting for transfers between devices: 1.99 us -> none  [the longest x4 1.97 us: padded_2(): lax.ppermute(head, axis, [((i + 1) % count, i) for i in range(ends)])]
  transfers between devices with their start and end apart: 11 -> 0, of which waited for: 4 -> 0; matrix products, arithmetic and copies ran while one was open for 9% -> 0% of each run, Pallas kernels for 0% -> 0%
where the time goes in v1:
time: 41.4 us; the launch traced here: 41.2 us
  Pallas kernels  34 us (82%)
  local copies, waits for them, and re-layouts  5.7 us (14%)
  other arithmetic  0.76 us (2%)
  between operations  0.68 us (2%)
    pallas_call x1, Pallas kernels, local(): pl.pallas_call(functools.partial(kernel, (n_tile, n_dp, share, chunk, sca...  34 us
    unnamed x10, local copies, waits for them, and re-layouts  4.37 us

profile of v1, /device:TPU:0, one launch (start us, length us, event | category | flops | bytes accessed | tf_op | source)
XLA Modules:
  0.0 41.2 jit_solution(2606260860430659775)
XLA Ops:
  0.6 0.0 copy-start
  0.6 0.8 %multiply_bitcast_fusion = bf16[2,8,4,128]{3,2,0,1:T(4,128)(2,1)S(1)} fusion(bf16[1,8,2,4,128]{4,3,2,1,0:T(4,128)(2,1)} %param.9), kind=kLoop, calls=%fused_computation.3 | loop fusion | flops 8192 | bytes 32768 | tf_op jit(solution)/shard_map/mul | solution.py:329
  1.5 0.0 copy-done
  1.5 0.0 copy-start.3
  1.5 0.6 %copy-done.3 = s32[1,8]{1,0:T(1,128)S(1)} copy-done((s32[1,8]{1,0:T(1,128)S(1)}, s32[1,8]{1,0:T(1,128)}, u32[]{:S(2)}) %copy-start.3) | copy-done | bytes 56
  2.1 0.0 copy-start.1
  2.1 1.2 %copy-done.1 = bf16[3456,128]{1,0:T(8,128)(2,1)S(1)} copy-done((bf16[3456,128]{1,0:T(8,128)(2,1)S(1)}, bf16[3456,128]{1,0:T(8,128)(2,1)}, u32[]{:S(2)}) %copy-start.1) | copy-done | bytes 884760
  3.3 0.0 copy-start.2
  3.3 1.2 %copy-done.2 = bf16[3456,128]{1,0:T(8,128)(2,1)S(1)} copy-done((bf16[3456,128]{1,0:T(8,128)(2,1)S(1)}, bf16[3456,128]{1,0:T(8,128)(2,1)}, u32[]{:S(2)}) %copy-start.2) | copy-done | bytes 884760
  4.5 34.0 %shard_map.84 = (f32[64,128]{1,0:T(8,128)S(1)}, f32[256,128]{1,0:T(8,128)S(1)}, f32[432,128]{1,0:T(8,128)S(1)}, f32[432,128]{1,0:T(8,128)S(1)}) custom-call(s32[1,8]{1,0:T(1,128)S(1)} %copy-done.3, bf16[4,64,128]{2,1,0:T(8,128)(2,1)S(1)} %copy_bitcast_fusion.1.x_in, bf16[3456,128]{1,0:T(8,128)(2,1)S(1)} %copy-done.1, bf16[3456,128]{1,0:T(8,128)(2,1)S(1)} %copy-done.2, ...), custom_call_target="tpu_custom_call" | custom-call | tf_op jit(solution)/shard_map/pallas_call | solution.py:335
  38.5 0.6 %copy.17 = f32[2,8,4,128]{3,2,0,1:T(4,128)} copy(f32[2,8,4,128]{3,2,1,0:T(4,128)S(1)} %bitcast.26) | data formatting | bytes 65536 | tf_op jit(solution)/shard_map/reshape | solution.py:375
  39.1 0.7 %copy.16 = f32[4,8,8,128]{3,2,0,1:T(8,128)} copy(f32[4,8,8,128]{3,2,1,0:T(8,128)S(1)} %bitcast.25) | data formatting | bytes 262144 | tf_op jit(solution)/shard_map/reshape | solution.py:376
  39.8 0.7 %copy.20 = f32[432,128]{1,0:T(8,128)} copy(f32[432,128]{1,0:T(8,128)S(1)} %get-tuple-element.18) | data formatting | bytes 442368
  40.5 0.7 %copy.21 = f32[432,128]{1,0:T(8,128)} copy(f32[432,128]{1,0:T(8,128)S(1)} %get-tuple-element.19) | data formatting | bytes 442368
  (3 shorter events, 0.0 us)
Async XLA Ops:
  0.6 0.8 %copy-start = (bf16[1,8,4,8,128]{4,3,2,1,0:T(8,128)(2,1)S(1)}, bf16[1,8,4,8,128]{4,3,2,1,0:T(8,128)(2,1)}, u32[]{:S(2)}) copy-start(bf16[1,8,4,8,128]{4,3,2,1,0:T(8,128)(2,1)} %param.5) | copy-start | bytes 196612
  1.5 0.7 %copy-start.3 = (s32[1,8]{1,0:T(1,128)S(1)}, s32[1,8]{1,0:T(1,128)}, u32[]{:S(2)}) copy-start(s32[1,8]{1,0:T(1,128)} %seg.1) | copy-start | bytes 100
  2.1 1.2 %copy-start.1 = (bf16[3456,128]{1,0:T(8,128)(2,1)S(1)}, bf16[3456,128]{1,0:T(8,128)(2,1)}, u32[]{:S(2)}) copy-start(bf16[3456,128]{1,0:T(8,128)(2,1)} %w1.1) | copy-start | bytes 2654212
  3.3 1.2 %copy-start.2 = (bf16[3456,128]{1,0:T(8,128)(2,1)S(1)}, bf16[3456,128]{1,0:T(8,128)(2,1)}, u32[]{:S(2)}) copy-start(bf16[3456,128]{1,0:T(8,128)(2,1)} %w2.1) | copy-start | bytes 2654212

commit v2 on v1

--- a/solution.py
+++ b/solution.py
@@ -64,17 +64,16 @@
 
 def kernel(
     cfg,
-    seg, x_in, w1, w2, g_in,
+    seg, x_hbm, w1_hbm, w2_hbm, g_in,
     pooled, in_grad, out1, out2,
-    x_halo, g_halo, cols_x, cols_h, cols_g, cols_a, w1t, w2t, pool_tmp,
-    flat1, flat2, recv_a, sum_a, send_b, recv_b, sum_b, send_c, recv_c, fin,
+    x_in, w1, w2, in_sem, x_halo, g_halo, cols_x, cols_h, cols_g, cols_a, w1t, w2t, pool_tmp,
+    flat1, flat2, send_a, recv_a, sum_a, send_b, recv_b, sum_b, send_c, recv_c, fin,
     h_send, h_recv, a_send, a_recv, b_send, b_recv, c_send, c_recv, d_send, d_recv,
 ):
     n_tile, n_dp, share, chunk, scale = cfg
     n_z = n_tile // 2
-    rows, slab, ch = x_in.shape
-    frames = seg.shape[1]
-    cols = slab // frames
+    rows, frames, cols, ch = x_in.shape
+    slab = frames * cols
     tile = lax.axis_index("tile")
     dp = lax.axis_index("dp")
     core = lax.rem(tile, 2)
@@ -82,6 +81,16 @@
     flats = (flat1, flat2)
     outs = (out1, out2)
 
+    load_x = [
+        pltpu.make_async_copy(x_hbm.at[0, :, r], x_in.at[r], in_sem.at[2 + r]) for r in range(rows)
+    ]
+    load_w1 = pltpu.make_async_copy(w1_hbm, w1, in_sem.at[0])
+    load_w2 = pltpu.make_async_copy(w2_hbm, w2, in_sem.at[1])
+    for copy in load_x:
+        copy.start()
+    load_w1.start()
+    load_w2.start()
+
     barrier = pltpu.get_barrier_semaphore()
 
     def greet(peer):
@@ -106,9 +115,11 @@
         for tap in range(27):
             dst[tap * ch : (tap + 1) * ch, :] = src[tap * ch : (tap + 1) * ch, :].T
 
-    flip(w2, w2t)
     for g in range(2):
-        sum_a[g, :, share:, :] = jnp.zeros((n_z, sum_a.shape[2] - share, ch), F32)
+        if sum_a.shape[2] > share:
+            sum_a[g, :, share:, :] = jnp.zeros((n_z, sum_a.shape[2] - share, ch), F32)
+        if send_a.shape[2] > share:
+            send_a[g, :, share:, :] = jnp.zeros((n_z, send_a.shape[2] - share, ch), BF16)
 
     @pl.when(tile == 0)
     def _():
@@ -120,6 +131,8 @@
         x_halo[1] = jnp.zeros(x_halo.shape[1:], BF16)
         g_halo[1] = jnp.zeros(g_halo.shape[1:], BF16)
 
+    for copy in load_x:
+        copy.wait()
     beside = jnp.where(tile > 0, 1, 0) + jnp.where(tile < n_tile - 1, 1, 0)
     pl.semaphore_wait(barrier, n_dp - 1 + n_z - 1 + beside)
 
@@ -152,6 +165,9 @@
         for copy in halo(1):
             copy.start()
 
+    load_w1.wait()
+    load_w2.wait()
+    flip(w2, w2t)
     flip(w1, w1t)
     same = [None]
     for t in range(1, 3):
@@ -179,10 +195,9 @@
 
     mine = x_in[...].astype(F32)
     x_all = jnp.concatenate([x_halo[0].astype(F32), mine, x_halo[1].astype(F32)], axis=0)
-    fill_columns(cols_x, four(x_all), same, False)
+    fill_columns(cols_x, x_all, same, False)
     g_all = jnp.concatenate([g_halo[0], g_in[...], g_halo[1]], axis=0).astype(F32)
     g_all = jnp.stack([g_all, g_all], axis=1).reshape(2 * g_all.shape[0], slab, ch)
-    fill_columns(cols_g, four(g_all), same, True)
 
     wide = rows + 2
     first = conv_dots(cols_x, w1, 0, wide, slab, False)
@@ -193,10 +208,6 @@
     def edges(v):
         v = v.reshape(wide, slab, ch)
         return jnp.concatenate([v[:1] * top, v[1:-1], v[-1:] * low], axis=0)
-
-    hidden_grad = conv_dots(cols_g, w2t, 0, wide, slab, True)
-    act = edges(hidden_grad * sigma * (1.0 + first * (1.0 - sigma)))
-    act_own = act[1 : 1 + rows].reshape(rows * slab, ch).astype(BF16)
 
     def kernel_grad(flat, cols_ref, start, g):
         for t in range(3):
@@ -212,7 +223,7 @@
     def copies_a(g):
         return [
             pltpu.make_async_remote_copy(
-                src_ref=flats[g].at[pl.ds(pl.multiple_of((2 * k + 1 - core) * share, 8), share)],
+                src_ref=send_a.at[g, k],
                 dst_ref=recv_a.at[g, k],
                 send_sem=a_send.at[g, k], recv_sem=a_recv.at[g, k],
                 device_id={"tile": tile + 1 - 2 * core}, device_id_type=MESH,
@@ -265,7 +276,7 @@
         wait(copies_a(g))
         for k in range(n_z):
             own = flats[g][pl.ds(pl.multiple_of((2 * k + core) * share, 8), share), :]
-            sum_a[g, k, 0:share, :] = own + recv_a[g, k]
+            sum_a[g, k, 0:share, :] = own + recv_a[g, k, 0:share].astype(F32)
         for i in range(1, n_dp):
             send_b[g, i - 1] = sum_a[g, :, part(lax.rem(dp + i, n_dp)), :].astype(BF16)
         start(copies_b(g))
@@ -288,34 +299,60 @@
         fin[g, part(dp), :] = total * scale
         start(copies_d(g))
 
-    kernel_grad(flat1, cols_x, 1, act_own)
-    start(copies_a(0))
+    def step_a(g):
+        for k, copy in enumerate(copies_a(g)):
+            at = pl.ds(pl.multiple_of((2 * k + 1 - core) * share, 8), share)
+            send_a[g, k, 0:share, :] = flats[g][at, :].astype(BF16)
+            copy.start()
+
     hidden = edges(first * sigma)
     fill_columns(cols_h, four(hidden), same, False)
     g_own = g_all[2 : 2 + rows].reshape(rows * slab, ch)
     kernel_grad(flat2, cols_h, 0, g_own.astype(BF16))
-    start(copies_a(1))
+    step_a(1)
+    fill_columns(cols_g, four(g_all), same, True)
+    hidden_grad = conv_dots(cols_g, w2t, 0, wide, slab, True)
+    act = edges(hidden_grad * sigma * (1.0 + first * (1.0 - sigma)))
+    act_own = act[1 : 1 + rows].reshape(rows * slab, ch).astype(BF16)
+
+    step_b(1)
+    kernel_grad(flat1, cols_x, 1, act_own)
+    step_a(0)
+    fill_columns(cols_a, four(act), same, True)
     step_b(0)
-    step_b(1)
     second = conv_dots(cols_h, w2, 0, rows, slab, False)
-    summed = mine + second.reshape(rows, slab, ch)
+    summed = mine.reshape(rows, slab, ch) + second.reshape(rows, slab, ch)
     pairs = rows // 2
     for i in range(pairs):
         pool_tmp[i * slab : (i + 1) * slab, :] = summed[2 * i] + summed[2 * i + 1]
-    half = pairs * slab // 2
-    pooled[...] = 0.25 * (
-        pool_tmp[pl.ds(0, half, stride=2), :] + pool_tmp[pl.ds(1, half, stride=2), :]
-    )
-    fill_columns(cols_a, four(act), same, True)
+    for i in range(pairs):
+        for f in range(frames):
+            at = i * slab + f * cols
+            pooled[0, f, i] = 0.25 * (
+                pool_tmp[pl.ds(at, cols // 2, stride=2), :]
+                + pool_tmp[pl.ds(at + 1, cols // 2, stride=2), :]
+            )
+    step_c(1)
+    back = conv_dots(cols_a, w1t, 0, rows, slab, True)
+    total = (g_own + back).reshape(rows, frames, cols, ch)
+    for r in range(rows):
+        in_grad[0, :, r] = total[r]
     step_c(0)
-    back = conv_dots(cols_a, w1t, 0, rows, slab, True)
-    in_grad[...] = g_own + back
-    step_c(1)
+    step_d(1)
     step_d(0)
-    step_d(1)
-    for g in range(2):
+    for g in (1, 0):
         wait(copies_d(g))
         outs[g][...] = fin[g, 0:share, :]
+
+
+def hand_on(*refs):
+    count = len(refs) // 2
+    sems = refs[-1]
+    copies = [pltpu.make_async_copy(refs[i], refs[count + i], sems.at[i]) for i in range(count)]
+    for copy in copies:
+        copy.start()
+    for copy in copies:
+        copy.wait()
 
 
 def local(n_tile, n_dp, clip_frames, segments, weight_first, weight_second, cotangent):
@@ -325,25 +362,30 @@
     share = taps // n_tile
     chunk = up16(-(-share // n_dp))
     n_z = n_tile // 2
-    x = clip_frames[0].transpose(1, 0, 2, 3).reshape(rows, slab, ch)
     g = jnp.repeat(cotangent[0].transpose(1, 0, 2, 3), 2, axis=2) * jnp.bfloat16(0.25)
     g = g.reshape(rows // 2, slab, ch)
     scale = 1.0 / math.sqrt(n_dp * n_tile * rows * slab)
     vmem = pl.BlockSpec(memory_space=pltpu.VMEM)
     cells = rows * slab
     sem = pltpu.SemaphoreType.DMA
-    pooled, in_grad, first, second = pl.pallas_call(
+    anywhere = pl.BlockSpec(memory_space=pl.ANY)
+    shapes = (
+        jax.ShapeDtypeStruct((1, frames, rows // 2, cols // 2, ch), F32),
+        jax.ShapeDtypeStruct((1, frames, rows, cols, ch), F32),
+        jax.ShapeDtypeStruct((share, ch), F32),
+        jax.ShapeDtypeStruct((share, ch), F32),
+    )
+    results = pl.pallas_call(
         functools.partial(kernel, (n_tile, n_dp, share, chunk, scale)),
-        out_shape=(
-            jax.ShapeDtypeStruct((cells // 4, ch), F32),
-            jax.ShapeDtypeStruct((cells, ch), F32),
-            jax.ShapeDtypeStruct((share, ch), F32),
-            jax.ShapeDtypeStruct((share, ch), F32),
-        ),
-        in_specs=[pl.BlockSpec(memory_space=pltpu.SMEM)] + [vmem] * 4,
+        out_shape=shapes,
+        in_specs=[pl.BlockSpec(memory_space=pltpu.SMEM)] + [anywhere] * 3 + [vmem],
         out_specs=(vmem,) * 4,
         scratch_shapes=[
-            pltpu.VMEM((2, 2, slab, ch), BF16),
+            pltpu.VMEM((rows, frames, cols, ch), BF16),
+            pltpu.VMEM((taps, ch), BF16),
+            pltpu.VMEM((taps, ch), BF16),
+            sem((2 + rows,)),
+            pltpu.VMEM((2, 2, frames, cols, ch), BF16),
             pltpu.VMEM((2, 1, slab, ch), BF16),
             pltpu.VMEM(((rows + 4) * slab, 9 * ch), BF16),
             pltpu.VMEM(((rows + 2) * slab, 9 * ch), BF16),
@@ -354,7 +396,8 @@
             pltpu.VMEM((cells // 2, ch), F32),
             pltpu.VMEM((taps, ch), F32),
             pltpu.VMEM((taps, ch), F32),
-            pltpu.VMEM((2, n_z, share, ch), F32),
+            pltpu.VMEM((2, n_z, up16(share), ch), BF16),
+            pltpu.VMEM((2, n_z, up16(share), ch), BF16),
             pltpu.VMEM((2, n_z, n_dp * chunk, ch), F32),
             pltpu.VMEM((2, n_dp - 1, n_z, chunk, ch), BF16),
             pltpu.VMEM((2, n_dp - 1, n_z, chunk, ch), BF16),
@@ -371,10 +414,14 @@
         compiler_params=pltpu.CompilerParams(
             collective_id=0, has_side_effects=True, vmem_limit_bytes=50 * 1024 * 1024
         ),
-    )(segments, x, weight_first, weight_second, g)
-    pooled = pooled.reshape(rows // 2, frames, cols // 2, ch).transpose(1, 0, 2, 3)
-    in_grad = in_grad.reshape(rows, frames, cols, ch).transpose(1, 0, 2, 3)
-    return (pooled[None], in_grad[None], first, second)
+    )(segments, clip_frames, weight_first, weight_second, g)
+    return pl.pallas_call(
+        hand_on,
+        out_shape=shapes,
+        in_specs=[anywhere] * 4,
+        out_specs=(anywhere,) * 4,
+        scratch_shapes=[sem((4,))],
+    )(*results)
 
 
 def solution(mesh):

time: 41.4 us -> 60.1 us (1.45)
  Pallas kernels: 34 us -> 52.7 us
    pallas_call x0 -> x1, Pallas kernels: none -> 19.5 us  [local(): pl.pallas_call(hand_on, out_shape=shapes, in_specs=[anywhere] * 4, out_sp...]
    reshape x3 -> x0, local copies, waits for them, and re-layouts: 1.3 us -> none  [the longest x1 0.66 us: local(): in_grad = in_grad.reshape(rows, frames, cols, ch).transpose(1, 0, 2, 3)]
    unnamed x10 -> x16, local copies, waits for them, and re-layouts: 4.37 us -> 5.62 us
    pallas_call x1, Pallas kernels: 34 us -> 33.2 us  [local(): pl.pallas_call(functools.partial(kernel, (n_tile, n_dp, share, chunk, sca...]
where the time goes in v2:
time: 60.1 us; the launch traced here: 59.8 us
  Pallas kernels  52.7 us (88%)
  local copies, waits for them, and re-layouts  5.65 us (9%)
  other arithmetic  0.76 us (1%)
  between operations  0.69 us (1%)
    pallas_call x1, Pallas kernels, local(): pl.pallas_call(functools.partial(kernel, (n_tile, n_dp, share, chunk, sca...  33.2 us
    pallas_call x1, Pallas kernels, local(): pl.pallas_call(hand_on, out_shape=shapes, in_specs=[anywhere] * 4, out_sp...  19.5 us
    unnamed x16, local copies, waits for them, and re-layouts  5.62 us

profile of v2, /device:TPU:0, one launch (start us, length us, event | category | flops | bytes accessed | tf_op | source)
XLA Modules:
  0.0 59.8 jit_solution(11111362142077968190)
XLA Ops:
  0.6 0.0 copy-start.5
  0.6 0.8 %multiply_bitcast_fusion = bf16[2,8,4,128]{3,2,0,1:T(4,128)(2,1)S(1)} fusion(bf16[1,8,2,4,128]{4,3,2,1,0:T(4,128)(2,1)} %param.9), kind=kLoop, calls=%fused_computation | loop fusion | flops 8192 | bytes 32768 | tf_op jit(solution)/shard_map/mul | solution.py:365
  1.4 0.0 copy-start.7
  1.5 0.0 copy-done.5
  1.5 0.6 %copy-done.7 = s32[1,8]{1,0:T(1,128)S(1)} copy-done((s32[1,8]{1,0:T(1,128)S(1)}, s32[1,8]{1,0:T(1,128)}, u32[]{:S(2)}) %copy-start.7) | copy-done | bytes 56
  2.1 0.0 copy-start
  2.1 1.2 %copy-done = bf16[3456,128]{1,0:T(8,128)(2,1)S(1)} copy-done((bf16[3456,128]{1,0:T(8,128)(2,1)S(1)}, bf16[3456,128]{1,0:T(8,128)(2,1)}, u32[]{:S(2)}) %copy-start) | copy-done | bytes 884760
  3.3 0.0 copy-start.1
  3.3 1.2 %copy-done.1 = bf16[3456,128]{1,0:T(8,128)(2,1)S(1)} copy-done((bf16[3456,128]{1,0:T(8,128)(2,1)S(1)}, bf16[3456,128]{1,0:T(8,128)(2,1)}, u32[]{:S(2)}) %copy-start.1) | copy-done | bytes 884760
  4.4 33.2 %shard_map.84 = (f32[1,8,2,4,128]{4,3,2,1,0:T(4,128)S(1)}, f32[1,8,4,8,128]{4,3,2,1,0:T(8,128)S(1)}, f32[432,128]{1,0:T(8,128)S(1)}, f32[432,128]{1,0:T(8,128)S(1)}) custom-call(s32[1,8]{1,0:T(1,128)S(1)} %copy-done.7, bf16[1,8,4,8,128]{4,3,2,1,0:T(8,128)(2,1)S(1)} %copy-done.5, bf16[3456,128]{1,0:T(8,128)(2,1)S(1)} %copy-done, ...), custom_call_target="tpu_custom_call" | custom-call | tf_op jit(solution)/shard_map/pallas_call | solution.py:378
  37.7 0.0 copy-start.2
  37.7 0.7 %copy-done.2 = f32[432,128]{1,0:T(8,128)} copy-done((f32[432,128]{1,0:T(8,128)}, f32[432,128]{1,0:T(8,128)S(1)}, u32[]{:S(2)}) %copy-start.2) | copy-done | bytes 221208
  38.4 0.0 copy-start.3
  38.4 0.7 %copy-done.3 = f32[432,128]{1,0:T(8,128)} copy-done((f32[432,128]{1,0:T(8,128)}, f32[432,128]{1,0:T(8,128)S(1)}, u32[]{:S(2)}) %copy-start.3) | copy-done | bytes 221208
  39.1 0.0 copy-start.4
  39.1 0.6 %copy-done.4 = f32[1,8,4,8,128]{4,3,2,1,0:T(8,128)} copy-done((f32[1,8,4,8,128]{4,3,2,1,0:T(8,128)}, f32[1,8,4,8,128]{4,3,2,1,0:T(8,128)S(1)}, u32[]{:S(2)}) %copy-start.4) | copy-done | bytes 131096
  39.7 0.0 copy-start.6
  39.7 0.6 %copy-done.6 = f32[1,8,2,4,128]{4,3,2,1,0:T(4,128)} copy-done((f32[1,8,2,4,128]{4,3,2,1,0:T(4,128)}, f32[1,8,2,4,128]{4,3,2,1,0:T(4,128)S(1)}, u32[]{:S(2)}) %copy-start.6) | copy-done | bytes 32792
  40.3 19.5 %shard_map.85 = (f32[1,8,2,4,128]{4,3,2,1,0:T(4,128)}, f32[1,8,4,8,128]{4,3,2,1,0:T(8,128)}, f32[432,128]{1,0:T(8,128)}, f32[432,128]{1,0:T(8,128)}) custom-call(f32[1,8,2,4,128]{4,3,2,1,0:T(4,128)} %copy-done.6, f32[1,8,4,8,128]{4,3,2,1,0:T(8,128)} %copy-done.4, f32[432,128]{1,0:T(8,128)} %copy-done.2, f32[432,128]{1,0:T(8,128)} %copy-done.3), custom_call_target="tpu_custom_call" | custom-call | tf_op jit(solution)/shard_map/pallas_call | solution.py:418
  (2 shorter events, 0.0 us)
Async XLA Ops:
  0.6 0.8 %copy-start.5 = (bf16[1,8,4,8,128]{4,3,2,1,0:T(8,128)(2,1)S(1)}, bf16[1,8,4,8,128]{4,3,2,1,0:T(8,128)(2,1)}, u32[]{:S(2)}) copy-start(bf16[1,8,4,8,128]{4,3,2,1,0:T(8,128)(2,1)} %x_hbm.1) | copy-start | bytes 196612
  1.4 0.7 %copy-start.7 = (s32[1,8]{1,0:T(1,128)S(1)}, s32[1,8]{1,0:T(1,128)}, u32[]{:S(2)}) copy-start(s32[1,8]{1,0:T(1,128)} %seg.1) | copy-start | bytes 100
  2.1 1.2 %copy-start = (bf16[3456,128]{1,0:T(8,128)(2,1)S(1)}, bf16[3456,128]{1,0:T(8,128)(2,1)}, u32[]{:S(2)}) copy-start(bf16[3456,128]{1,0:T(8,128)(2,1)} %w1_hbm.1) | copy-start | bytes 2654212
  3.3 1.2 %copy-start.1 = (bf16[3456,128]{1,0:T(8,128)(2,1)S(1)}, bf16[3456,128]{1,0:T(8,128)(2,1)}, u32[]{:S(2)}) copy-start(bf16[3456,128]{1,0:T(8,128)(2,1)} %w2_hbm.1) | copy-start | bytes 2654212
  37.7 0.7 %copy-start.2 = (f32[432,128]{1,0:T(8,128)}, f32[432,128]{1,0:T(8,128)S(1)}, u32[]{:S(2)}) copy-start(f32[432,128]{1,0:T(8,128)S(1)} %get-tuple-element.10.refs_2_) | copy-start | bytes 663556
  38.4 0.7 %copy-start.3 = (f32[432,128]{1,0:T(8,128)}, f32[432,128]{1,0:T(8,128)S(1)}, u32[]{:S(2)}) copy-start(f32[432,128]{1,0:T(8,128)S(1)} %get-tuple-element.11.refs_3_) | copy-start | bytes 663556
  39.1 0.6 %copy-start.4 = (f32[1,8,4,8,128]{4,3,2,1,0:T(8,128)}, f32[1,8,4,8,128]{4,3,2,1,0:T(8,128)S(1)}, u32[]{:S(2)}) copy-start(f32[1,8,4,8,128]{4,3,2,1,0:T(8,128)S(1)} %get-tuple-element.9.refs_1_) | copy-start | bytes 393220
  39.7 0.6 %copy-start.6 = (f32[1,8,2,4,128]{4,3,2,1,0:T(4,128)}, f32[1,8,2,4,128]{4,3,2,1,0:T(4,128)S(1)}, u32[]{:S(2)}) copy-start(f32[1,8,2,4,128]{4,3,2,1,0:T(4,128)S(1)} %get-tuple-element.8.refs_0_) | copy-start | bytes 98308

commit v3 on v2

--- a/solution.py
+++ b/solution.py
@@ -345,16 +345,6 @@
         outs[g][...] = fin[g, 0:share, :]
 
 
-def hand_on(*refs):
-    count = len(refs) // 2
-    sems = refs[-1]
-    copies = [pltpu.make_async_copy(refs[i], refs[count + i], sems.at[i]) for i in range(count)]
-    for copy in copies:
-        copy.start()
-    for copy in copies:
-        copy.wait()
-
-
 def local(n_tile, n_dp, clip_frames, segments, weight_first, weight_second, cotangent):
     _, frames, rows, cols, ch = clip_frames.shape
     slab = frames * cols
@@ -368,7 +358,7 @@
     vmem = pl.BlockSpec(memory_space=pltpu.VMEM)
     cells = rows * slab
     sem = pltpu.SemaphoreType.DMA
-    anywhere = pl.BlockSpec(memory_space=pl.ANY)
+    anywhere = pl.BlockSpec(memory_space=pltpu.HBM)
     shapes = (
         jax.ShapeDtypeStruct((1, frames, rows // 2, cols // 2, ch), F32),
         jax.ShapeDtypeStruct((1, frames, rows, cols, ch), F32),
@@ -415,13 +405,7 @@
             collective_id=0, has_side_effects=True, vmem_limit_bytes=50 * 1024 * 1024
         ),
     )(segments, clip_frames, weight_first, weight_second, g)
-    return pl.pallas_call(
-        hand_on,
-        out_shape=shapes,
-        in_specs=[anywhere] * 4,
-        out_specs=(anywhere,) * 4,
-        scratch_shapes=[sem((4,))],
-    )(*results)
+    return tuple(results)
 
 
 def solution(mesh):

time: 60.1 us -> 40.6 us (0.68)
  Pallas kernels: 52.7 us -> 33.2 us
    pallas_call x1 -> x0, Pallas kernels: 19.5 us -> none  [local(): pl.pallas_call(hand_on, out_shape=shapes, in_specs=[anywhere] * 4, out_sp...]
    unnamed x16 -> x12, local copies, waits for them, and re-layouts: 5.62 us -> 5.63 us
where the time goes in v3:
time: 40.6 us; the launch traced here: 40.3 us
  Pallas kernels  33.2 us (82%)
  local copies, waits for them, and re-layouts  5.66 us (14%)
  other arithmetic  0.76 us (2%)
  between operations  0.68 us (2%)
    pallas_call x1, Pallas kernels, local(): pl.pallas_call(functools.partial(kernel, (n_tile, n_dp, share, chunk, sca...  33.2 us
    unnamed x12, local copies, waits for them, and re-layouts  5.63 us

profile of v3, /device:TPU:0, one launch (start us, length us, event | category | flops | bytes accessed | tf_op | source)
XLA Modules:
  0.0 40.3 jit_solution(8909111648645172535)
XLA Ops:
  0.6 0.0 copy-start.2
  0.6 0.8 %multiply_bitcast_fusion = bf16[2,8,4,128]{3,2,0,1:T(4,128)(2,1)S(1)} fusion(bf16[1,8,2,4,128]{4,3,2,1,0:T(4,128)(2,1)} %param.9), kind=kLoop, calls=%fused_computation | loop fusion | flops 8192 | bytes 32768 | tf_op jit(solution)/shard_map/mul | solution.py:355
  1.4 0.0 copy-start.3
  1.5 0.0 copy-done.2
  1.5 0.6 %copy-done.3 = s32[1,8]{1,0:T(1,128)S(1)} copy-done((s32[1,8]{1,0:T(1,128)S(1)}, s32[1,8]{1,0:T(1,128)}, u32[]{:S(2)}) %copy-start.3) | copy-done | bytes 56
  2.1 0.0 copy-start
  2.1 1.2 %copy-done = bf16[3456,128]{1,0:T(8,128)(2,1)S(1)} copy-done((bf16[3456,128]{1,0:T(8,128)(2,1)S(1)}, bf16[3456,128]{1,0:T(8,128)(2,1)}, u32[]{:S(2)}) %copy-start) | copy-done | bytes 884760
  3.3 0.0 copy-start.1
  3.3 1.2 %copy-done.1 = bf16[3456,128]{1,0:T(8,128)(2,1)S(1)} copy-done((bf16[3456,128]{1,0:T(8,128)(2,1)S(1)}, bf16[3456,128]{1,0:T(8,128)(2,1)}, u32[]{:S(2)}) %copy-start.1) | copy-done | bytes 884760
  4.4 33.2 %shard_map.84 = (f32[1,8,2,4,128]{4,3,2,1,0:T(4,128)S(1)}, f32[1,8,4,8,128]{4,3,2,1,0:T(8,128)S(1)}, f32[432,128]{1,0:T(8,128)S(1)}, f32[432,128]{1,0:T(8,128)S(1)}) custom-call(s32[1,8]{1,0:T(1,128)S(1)} %copy-done.3, bf16[1,8,4,8,128]{4,3,2,1,0:T(8,128)(2,1)S(1)} %copy-done.2, bf16[3456,128]{1,0:T(8,128)(2,1)S(1)} %copy-done, ...), custom_call_target="tpu_custom_call" | custom-call | tf_op jit(solution)/shard_map/pallas_call | solution.py:368
  37.7 0.6 %copy.14 = f32[1,8,2,4,128]{4,3,2,1,0:T(4,128)} copy(f32[1,8,2,4,128]{4,3,2,1,0:T(4,128)S(1)} %get-tuple-element.8) | data formatting | bytes 65536
  38.3 0.7 %copy.15 = f32[1,8,4,8,128]{4,3,2,1,0:T(8,128)} copy(f32[1,8,4,8,128]{4,3,2,1,0:T(8,128)S(1)} %get-tuple-element.9) | data formatting | bytes 262144
  39.0 0.7 %copy.16 = f32[432,128]{1,0:T(8,128)} copy(f32[432,128]{1,0:T(8,128)S(1)} %get-tuple-element.10) | data formatting | bytes 442368
  39.6 0.7 %copy.17 = f32[432,128]{1,0:T(8,128)} copy(f32[432,128]{1,0:T(8,128)S(1)} %get-tuple-element.11) | data formatting | bytes 442368
  (2 shorter events, 0.0 us)
Async XLA Ops:
  0.6 0.8 %copy-start.2 = (bf16[1,8,4,8,128]{4,3,2,1,0:T(8,128)(2,1)S(1)}, bf16[1,8,4,8,128]{4,3,2,1,0:T(8,128)(2,1)}, u32[]{:S(2)}) copy-start(bf16[1,8,4,8,128]{4,3,2,1,0:T(8,128)(2,1)} %x_hbm.1) | copy-start | bytes 196612
  1.4 0.7 %copy-start.3 = (s32[1,8]{1,0:T(1,128)S(1)}, s32[1,8]{1,0:T(1,128)}, u32[]{:S(2)}) copy-start(s32[1,8]{1,0:T(1,128)} %seg.1) | copy-start | bytes 100
  2.1 1.2 %copy-start = (bf16[3456,128]{1,0:T(8,128)(2,1)S(1)}, bf16[3456,128]{1,0:T(8,128)(2,1)}, u32[]{:S(2)}) copy-start(bf16[3456,128]{1,0:T(8,128)(2,1)} %w1_hbm.1) | copy-start | bytes 2654212
  3.3 1.2 %copy-start.1 = (bf16[3456,128]{1,0:T(8,128)(2,1)S(1)}, bf16[3456,128]{1,0:T(8,128)(2,1)}, u32[]{:S(2)}) copy-start(bf16[3456,128]{1,0:T(8,128)(2,1)} %w2_hbm.1) | copy-start | bytes 2654212
